TPU v7x, 32 devices: a whole 2x2x4 slice. The times are simulated.
32 devices in a mesh: ctx: 8 (over y, x, core), tp: 4 (over z).
Axes of the slice: x: 2, y: 2, z: 4, core: 2. Of those that a mesh axis runs over, the one named last changes fastest.
Arguments:
- features: bfloat16 [3, 2048, 8192], P(None, 'ctx', 'tp'), may hold values from -6 to 6
- short_taps: bfloat16 [3, 512, 7], P(None, 'tp'), may hold values from -2 to 2
- long_taps: bfloat16 [512, 128], P('tp'), may hold values from -0.5 to 0.5
- skip_gain: bfloat16 [8192], P('tp'), may hold values from -4 to 4
- cotangent: bfloat16 [2048, 8192], P('ctx', 'tp'), may hold values from -6 to 6
Outputs:
- gated: bfloat16 [2048, 8192], P('ctx', 'tp')
- feature_grad: bfloat16 [3, 2048, 8192], P(None, 'ctx', 'tp')
- short_grad: float32 [3, 512, 7], P(None, 'tp')
- long_grad: float32 [512, 128], P('tp')
- skip_grad: float32 [8192], P('tp')
All inputs are finite; a program needn't handle non-finite values.
Results may differ from a plain program's by a relative error of at most 0.0074.
Values may be sent and summed in bfloat16 or wider, within the bound.
A program may use at most 128 MiB of HBM per device.

v0:
```python
import math

import jax
import jax.numpy as jnp
from jax import lax
from jax.sharding import PartitionSpec as P


def passed_along(block, axis, distance):
    devices = range(lax.axis_size(axis))
    route = [(i - distance, i) for i in devices if i - distance in devices]
    return lax.ppermute(block, axis, route)


def settle(values):
    return lax.optimization_barrier(values)


def short_filter(padded, taps, rows):
    total = jnp.zeros((padded.shape[0], rows, padded.shape[2]), jnp.float32)
    for offset in range(7):
        total = total + taps[:, None, :, offset] * padded[:, 6 - offset : 6 - offset + rows].astype(
            jnp.float32
        )
    return total


def toeplitz_blocks(filt):
    groups = filt.shape[0]
    extra = jnp.concatenate([filt, jnp.zeros((groups, 1), filt.dtype)], axis=1)
    row_pos = jnp.arange(128, dtype=jnp.int32)[:, None]
    col_pos = jnp.arange(256, dtype=jnp.int32)[None, :]
    shift_lag = row_pos + 128 - col_pos
    valid = (shift_lag >= 0) & (shift_lag < 128)
    picks = jnp.where(valid, shift_lag, 128)
    return jnp.take(extra, picks, axis=1)


def diagonal_sums(grid):
    groups = grid.shape[0]
    padded = jnp.pad(grid, ((0, 0), (0, 0), (0, 126)))
    flat = jnp.pad(padded.reshape(groups, 128 * 382), ((0, 0), (0, 128)))
    folded = flat.reshape(groups, 128, 383).sum(axis=1)
    return folded[:, 1:129][:, ::-1]


def to_blocks(rows_first, groups):
    return rows_first.T.reshape(groups, 16, rows_first.shape[0])


def body(features, short_taps, long_taps, skip_gain, cotangent):
    rows = features.shape[1]
    width = features.shape[2]
    groups = width // 16
    blocks = rows // 128
    taps = jnp.repeat(short_taps, 16, axis=1).astype(jnp.float32)
    gain = skip_gain.astype(jnp.float32)
    zero_row = jnp.zeros((1, width), jnp.bfloat16)
    bundle = jnp.concatenate([features[:, :133], cotangent[None, :133]], axis=0)
    received = passed_along(bundle, "ctx", -1)
    edge = passed_along(features[:, rows - 6 :], "ctx", 1)
    padded = jnp.concatenate([edge, features], axis=1)
    mixed = settle(short_filter(padded, taps, rows).astype(jnp.bfloat16))
    product = settle(
        (mixed[1].astype(jnp.float32) * mixed[2].astype(jnp.float32)).astype(jnp.bfloat16)
    )
    tail = passed_along(product[rows - 127 :], "ctx", 1)
    extended = jnp.concatenate([zero_row, tail, product], axis=0)
    query = mixed[0].astype(jnp.float32)
    key = mixed[1].astype(jnp.float32)
    value = mixed[2].astype(jnp.float32)
    kernel = toeplitz_blocks(long_taps)
    earlier = kernel[:, :, :128]
    current = kernel[:, :, 128:]
    ext_t = to_blocks(extended, groups)
    before = ext_t[:, :, :rows].reshape(groups, 16 * blocks, 128)
    present = ext_t[:, :, 128:].reshape(groups, 16 * blocks, 128)
    conv = jnp.einsum("gts,gns->gnt", earlier, before, preferred_element_type=jnp.float32)
    conv = conv + jnp.einsum("gts,gns->gnt", current, present, preferred_element_type=jnp.float32)
    conv = conv.reshape(width, rows).T
    prod_f = product.astype(jnp.float32)
    inner = conv + gain * prod_f
    gated = (query * inner).astype(jnp.bfloat16)
    grad_in = cotangent.astype(jnp.float32)
    grad_query = grad_in * inner
    grad_inner = settle((grad_in * query).astype(jnp.bfloat16))
    next_feat = received[:3]
    next_cot = received[3].astype(jnp.float32)
    next_padded = jnp.concatenate([features[:, rows - 6 :], next_feat], axis=1)
    next_mixed = settle(short_filter(next_padded, taps, 133).astype(jnp.bfloat16))
    next_query = next_mixed[0].astype(jnp.float32)
    next_key = next_mixed[1, :6].astype(jnp.float32)
    next_value = next_mixed[2, :6].astype(jnp.float32)
    next_product = settle((next_key * next_value).astype(jnp.bfloat16)).astype(jnp.float32)
    next_inner_grad = settle((next_cot * next_query).astype(jnp.bfloat16))
    ahead = next_inner_grad[:127]
    filt = jnp.repeat(long_taps, 16, axis=0).astype(jnp.float32)
    lead = jnp.arange(6, dtype=jnp.int32)[:, None]
    lag = jnp.arange(128, dtype=jnp.int32)[None, :]
    window = jnp.concatenate([product[rows - 127 :].astype(jnp.float32), next_product], axis=0)
    next_conv = jnp.einsum("tjc,cj->tc", window[127 + lead - lag], filt)
    next_inner = next_conv + gain * next_product
    next_grad_query = next_cot[:6] * next_inner
    inner_next_f = next_inner_grad.astype(jnp.float32)
    next_back = jnp.einsum("tjc,cj->tc", inner_next_f[lead + lag], filt)
    next_grad_product = settle((next_back + gain * inner_next_f[:6]).astype(jnp.bfloat16)).astype(
        jnp.float32
    )
    head = settle(
        jnp.stack(
            [next_grad_query, next_grad_product * next_value, next_grad_product * next_key], axis=0
        ).astype(jnp.bfloat16)
    )
    later = jnp.concatenate([grad_inner, ahead, zero_row], axis=0)
    later_t = to_blocks(later, groups)
    this_block = later_t[:, :, :rows].reshape(groups, 16 * blocks, 128)
    next_block = later_t[:, :, 128:].reshape(groups, 16 * blocks, 128)
    back = jnp.einsum("gts,gnt->gns", current, this_block, preferred_element_type=jnp.float32)
    back = back + jnp.einsum(
        "gts,gnt->gns", earlier, next_block, preferred_element_type=jnp.float32
    )
    back = back.reshape(width, rows).T
    inner_f = grad_inner.astype(jnp.float32)
    grad_product = settle((back + gain * inner_f).astype(jnp.bfloat16))
    product_g = grad_product.astype(jnp.float32)
    grad_mixed = settle(
        jnp.stack([grad_query, product_g * value, product_g * key], axis=0).astype(jnp.bfloat16)
    )
    trailing = jnp.concatenate([grad_mixed, head], axis=1)
    feature_grad = jnp.zeros((3, rows, width), jnp.float32)
    for offset in range(7):
        feature_grad = feature_grad + taps[:, None, :, offset] * trailing[
            :, offset : offset + rows
        ].astype(jnp.float32)
    grid = jnp.concatenate(
        [
            jnp.einsum("gnt,gns->gts", this_block, before, preferred_element_type=jnp.float32),
            jnp.einsum("gnt,gns->gts", this_block, present, preferred_element_type=jnp.float32),
        ],
        axis=2,
    )
    long_local = diagonal_sums(grid)
    skip_local = jnp.sum(inner_f * prod_f, axis=0)
    mixed_g = grad_mixed.astype(jnp.float32)
    short_all = jnp.stack(
        [
            jnp.sum(mixed_g * padded[:, 6 - offset : 6 - offset + rows].astype(jnp.float32), axis=1)
            for offset in range(7)
        ],
        axis=-1,
    )
    short_local = short_all.reshape(3, groups, 16, 7).sum(axis=2)
    long_sum, skip_sum, short_sum = lax.psum((long_local, skip_local, short_local), "ctx")
    total = rows * lax.axis_size("ctx")
    group_scale = 1.0 / math.sqrt(16.0 * total)
    token_scale = 1.0 / math.sqrt(1.0 * total)
    return (
        gated,
        feature_grad.astype(jnp.bfloat16),
        short_sum * group_scale,
        long_sum * group_scale,
        skip_sum * token_scale,
    )


def solution(mesh):
    placed = (P(None, "ctx", "tp"), P(None, "tp", None), P("tp", None), P("tp"), P("ctx", "tp"))
    return jax.shard_map(
        body,
        mesh=mesh,
        in_specs=placed,
        out_specs=(
            P("ctx", "tp"),
            P(None, "ctx", "tp"),
            P(None, "tp", None),
            P("tp", None),
            P("tp"),
        ),
        check_vma=False,
    )
```

profile of v0, /device:TPU:0, one launch (start us, length us, event | category | flops | bytes accessed | tf_op | source)
XLA Modules:
  0.0 509.6 jit_solution(9779534980435420364)
XLA Ops:
  19.8 114.9 %gather_fusion = bf16[32768,128]{1,0:T(8,128)(2,1)} fusion(bf16[128,129]{0,1:T(8,128)(2,1)S(1)} %concatenate.30, s32[32768]{0:T(1024)S(1)} %broadcast_clamp_fusion), kind=kCustom, calls=%fused_computation | custom fusion | bytes 16908288 | tf_op jit(solution)/shard_map/jit(_take)/gather | solution.py:36
  134.7 12.6 %copy.89 = bf16[128,256,128]{1,0,2:T(8,128)(2,1)} copy(bf16[128,256,128]{2,1,0:T(8,128)(2,1)} %bitcast.132) | data formatting | bytes 16777216 | tf_op jit(solution)/shard_map/jit(_take)/gather | solution.py:36
  147.4 7.7 %select_bitcast_fusion = bf16[128,128,256]{2,1,0:T(8,128)(2,1)} fusion(bf16[128,256,128]{1,0,2:T(8,128)(2,1)} %copy.89, pred[128,256]{1,0:T(8,128)(4,1)S(1)} %fusion.71), kind=kLoop, calls=%fused_computation.12 | loop fusion | flops 4194304 | bytes 16809984 | tf_op jit(solution)/shard_map/jit(_take)/select_n | solution.py:36
  155.8 6.9 %fusion.6 = bf16[3,256,2048]{2,1,0:T(8,128)(2,1)S(1)} fusion(bf16[3,256,2048]{2,1,0:T(8,128)(2,1)S(1)} %copy-done.4, bf16[3,6,2048]{2,1,0:T(8,128)(2,1)} %copy-done.17, f32[3,2048]{1,0:T(4,128)S(1)} %get-tuple-element.55, f32[3,2048]{1,0:T(4,128)S(1)} %get-tuple-element.56, f32[3,2048]{1,0:T(4,128)S(1)} %get-tuple-element.57, ...), kind=kLoop, calls=%fused_computation.36 | loop fusion | flops 61341696 | bytes 6537216 | tf_op jit(solution)/shard_map/convert_element_type | solution.py:63
  165.7 6.1 %collective-permute-start.1 = (bf16[127,2048]{1,0:T(8,128)(2,1)}, bf16[127,2048]{1,0:T(8,128)(2,1)}, u32[]{:S(2)}, u32[]{:S(2)}) collective-permute-start(bf16[127,2048]{1,0:T(8,128)(2,1)} %get-tuple-element.45), channel_id=1, source_target_pairs={{0,4},{4,8},{8,12},{12,16},{16,20},{20,24},{24,28},{1,5},{5,9},{9,... | collective-permute-start | bytes 1560584 | tf_op jit(solution)/shard_map/ppermute | solution.py:12
  188.3 4.9 fusion.23
  193.2 5.9 %fusion.54 = f32[128,32,128]{2,1,0:T(8,128)} fusion(f32[128,32,128]{2,1,0:T(8,128)S(1)} %fusion.23, bf16[128,32,128]{2,1,0:T(8,128)(2,1)S(1)} %copy-done.8, bf16[128,128,256]{2,1,0:T(8,128)(2,1)} %select_bitcast_fusion), kind=kOutput, calls=%fused_computation.112 | convolution fusion | flops 134742016 | bytes 9437184 | tf_op jit(solution)/shard_map/gts,gns->gnt/dot_general | solution.py:78
  226.1 4.8 fusion.21
  230.9 4.6 fusion.89
  235.4 4.6 fusion.88
  244.5 4.9 gather_fusion.1
  249.4 5.0 multiply_reduce_fusion.1
  258.5 5.1 fusion.57
  273.4 7.6 %fusion.13 = bf16[3,256,2048]{2,1,0:T(8,128)(2,1)} fusion(bf16[3,256,2048]{2,1,0:T(8,128)(2,1)S(1)} %pad_maximum_fusion.3, bf16[3,6,2048]{2,1,0:T(8,128)(2,1)S(1)} %pad_maximum_fusion.7, f32[3,2048]{1,0:T(4,128)S(1)} %get-tuple-element.55, f32[3,2048]{1,0:T(4,128)S(1)} %get-tuple-element.56, f32[3,2048]{1,0:T(4,128)S(1)} %get-tuple-element.57, ...), kind=kLoop, calls=%fused_computation.43 | loop fusion | flops 61341696 | bytes 6537216 | tf_op jit(solution)/shard_map/convert_element_type | solution.py:159
  281.0 6.7 %fusion.20 = (f32[3,2048]{1,0:T(4,128)S(1)}, f32[3,2048]{1,0:T(4,128)S(1)}, f32[3,2048]{1,0:T(4,128)S(1)}, f32[3,2048]{1,0:T(4,128)S(1)}, f32[3,2048]{1,0:T(4,12...) fusion(bf16[3,256,2048]{2,1,0:T(8,128)(2,1)S(1)} %pad_maximum_fusion.3, bf16[3,256,2048]{2,1,0:T(8,128)(2,1)S(1)} %copy-done.5, ...), kind=kLoop, calls=%fused_computation.50 | loop fusion | flops 62871552 | bytes 6537216 | tf_op jit(solution)/shard_map/reduce_sum | solution.py:147
  289.2 26.5 %all-reduce.3 = (f32[3,128,7]{1,0,2:T(4,128)S(1)}, f32[2048]{0:T(1024)S(1)}) all-reduce(f32[3,128,7]{1,0,2:T(4,128)S(1)} %reduce_sum.97, f32[2048]{0:T(1024)S(1)} %get-tuple-element.42), channel_id=1, replica_groups=mesh['ctx'=8,'tp'=4] {'ctx'}, use_global_device_ids=true, to_apply=%region_8.9 | all-reduce | flops 4736 | bytes 37888 | tf_op jit(solution)/shard_map/psum | solution.py:153
  315.7 11.7 %pad_maximum_fusion = f32[128,128,256]{1,2,0:T(8,128)} fusion(f32[128,128,128]{1,2,0:T(8,128)} %fusion.89, f32[128,128,128]{1,2,0:T(8,128)} %fusion.88), kind=kLoop, calls=%fused_computation.11 | loop fusion | flops 4194304 | bytes 33554432 | tf_op jit(solution)/shard_map/concatenate | solution.py:135
  327.4 17.5 %copy.101 = f32[128,128,256]{2,1,0:T(8,128)} copy(f32[128,128,256]{1,2,0:T(8,128)} %pad_maximum_fusion) | data formatting | bytes 33554432
  344.9 15.0 %pad.9.clone = f32[128,128,382]{2,1,0:T(8,128)} pad(f32[128,128,256]{2,1,0:T(8,128)} %copy.101, f32[]{:T(128)} %constant.17.clone.1), padding=0_0x0_0x0_126 | pad | bytes 41811972 | tf_op jit(solution)/shard_map/jit(_pad)/pad | solution.py:41
  359.8 26.9 %reshape.235 = f32[128,48896]{1,0:T(8,128)} reshape(f32[128,128,382]{2,1,0:T(8,128)} %pad.9.clone) | data formatting | bytes 50069504 | tf_op jit(solution)/shard_map/reshape | solution.py:42
  386.7 17.0 %pad.10 = f32[128,49024]{1,0:T(8,128)} pad(f32[128,48896]{1,0:T(8,128)} %reshape.235, f32[]{:T(128)} %constant.17.clone.1), padding=0_0x0_128 | pad | bytes 50135044 | tf_op jit(solution)/shard_map/jit(_pad)/pad | solution.py:42
  403.7 31.9 %reshape.236 = f32[128,128,383]{2,1,0:T(8,128)} reshape(f32[128,49024]{1,0:T(8,128)} %pad.10) | data formatting | bytes 50200576 | tf_op jit(solution)/shard_map/reshape | solution.py:43
  435.6 9.4 %reduce_sum.98 = f32[128,383]{1,0:T(8,128)S(1)} reduce(f32[128,128,383]{2,1,0:T(8,128)} %reshape.236, f32[]{:T(128)} %constant.17.clone.1), dimensions={1}, to_apply=%region_9.10 | reduce | flops 6226048 | bytes 25296388 | tf_op jit(solution)/shard_map/reduce_sum | solution.py:43
  447.1 53.8 %all-reduce.6.cloned.1.call-done = f32[128,128]{1,0:T(8,128)} async-done(((f32[128,128]{1,0:T(8,128)}), f32[128,128]{1,0:T(8,128)}) %all-reduce.6.cloned.1.call-update) | async-done | bytes 65552 | tf_op jit(solution)/shard_map/psum | solution.py:153
  (134 shorter events, 82.8 us)
Async XLA Ops:
  7.2 4.4 slice-start
  7.2 3.5 copy-start.16
  7.2 493.7 %all-reduce.6.cloned.1.call-start = ((), (), s32[]{:S(2)}) async-start(), calls=%async_computation | async-start | bytes 131072 | tf_op jit(solution)/shard_map/psum | solution.py:153
  8.3 146.8 %collective-permute-start = (bf16[3,6,2048]{2,1,0:T(8,128)(2,1)S(1)}, bf16[3,6,2048]{2,1,0:T(8,128)(2,1)S(1)}, u32[]{:S(2)}, u32[]{:S(2)}) collective-permute-start(bf16[3,6,2048]{2,1,0:T(8,128)(2,1)S(1)} %slice.173), channel_id=1, source_target_pairs={{0,4},{4,8},{8,12},{12,16},{16,20},{20,24},{24,28},{1,5},{5,9},{9,... | collective-permute-start | bytes 221192 | tf_op jit(solution)/shard_map/ppermute | solution.py:12
  13.0 5.2 %copy-start.19 = (bf16[128,128]{1,0:T(8,128)(2,1)S(1)}, bf16[128,128]{1,0:T(8,128)(2,1)}, u32[]{:S(2)}) copy-start(bf16[128,128]{1,0:T(8,128)(2,1)} %param.7) | copy-start | bytes 98308
  13.0 5.4 %copy-start.20 = (bf16[3,128,7]{1,2,0:T(8,128)(2,1)S(1)}, bf16[3,128,7]{1,2,0:T(8,128)(2,1)}, u32[]{:S(2)}) copy-start(bf16[3,128,7]{1,2,0:T(8,128)(2,1)} %param.6) | copy-start | bytes 16132
  16.6 192.7 %collective-permute-start.2 = (bf16[4,133,2048]{2,0,1:T(4,128)(2,1)}, bf16[4,133,2048]{2,0,1:T(4,128)(2,1)}, u32[]{:S(2)}, u32[]{:S(2)}) collective-permute-start(bf16[4,133,2048]{2,0,1:T(4,128)(2,1)} %pad_maximum_fusion.4), channel_id=1, source_target_pairs={{4,0},{8,4},{12,8},{16,12},{20,16},{24,20},{28,24},{5,1},{9,5},{13... | collective-permute-start | bytes 6537224 | tf_op jit(solution)/shard_map/ppermute | solution.py:12
  147.4 8.4 %copy-start.4 = (bf16[3,256,2048]{2,1,0:T(8,128)(2,1)S(1)}, bf16[3,256,2048]{2,1,0:T(8,128)(2,1)}, u32[]{:S(2)}) copy-start(bf16[3,256,2048]{2,1,0:T(8,128)(2,1)} %param.5) | copy-start | bytes 9437188
  162.6 42.2 %copy-start = (bf16[3,256,2048]{2,1,0:T(8,128)(2,1)}, bf16[3,256,2048]{2,1,0:T(8,128)(2,1)S(1)}, u32[]{:S(2)}) copy-start(bf16[3,256,2048]{2,1,0:T(8,128)(2,1)S(1)} %fusion.6) | copy-start | bytes 9437188
  162.7 10.3 %copy-start.21 = (bf16[2048]{0:T(1024)(128)(2,1)S(1)}, bf16[2048]{0:T(1024)(128)(2,1)}, u32[]{:S(2)}) copy-start(bf16[2048]{0:T(1024)(128)(2,1)} %param.8) | copy-start | bytes 12292
  163.1 1.3 copy-start.2
  165.7 9.8 %collective-permute-start.1 = (bf16[127,2048]{1,0:T(8,128)(2,1)}, bf16[127,2048]{1,0:T(8,128)(2,1)}, u32[]{:S(2)}, u32[]{:S(2)}) collective-permute-start(bf16[127,2048]{1,0:T(8,128)(2,1)} %get-tuple-element.45), channel_id=1, source_target_pairs={{0,4},{4,8},{8,12},{12,16},{16,20},{20,24},{24,28},{1,5},{5,9},{9,... | collective-permute-start | bytes 1560584 | tf_op jit(solution)/shard_map/ppermute | solution.py:12
  188.3 4.9 copy-start.8
  209.3 11.2 %copy-start.6 = (bf16[256,2048]{1,0:T(8,128)(2,1)}, bf16[256,2048]{1,0:T(8,128)(2,1)S(1)}, u32[]{:S(2)}) copy-start(bf16[256,2048]{1,0:T(8,128)(2,1)S(1)} %get-tuple-element.35) | copy-start | bytes 3145732
  226.1 4.8 copy-start.10
  230.9 4.6 copy-start.9
  240.1 4.3 copy-start.13
  244.5 4.9 copy-start.14
  254.4 4.1 copy-start.11
  263.6 5.9 %copy-start.3 = (bf16[256,2048]{1,0:T(8,128)(2,1)S(1)}, bf16[256,2048]{1,0:T(8,128)(2,1)}, u32[]{:S(2)}) copy-start(bf16[256,2048]{1,0:T(8,128)(2,1)} %copy-done.2) | copy-start | bytes 3145732
  263.6 5.9 %copy-start.7 = (bf16[256,2048]{1,0:T(8,128)(2,1)S(1)}, bf16[256,2048]{1,0:T(8,128)(2,1)}, u32[]{:S(2)}) copy-start(bf16[256,2048]{1,0:T(8,128)(2,1)} %copy-done.6) | copy-start | bytes 3145732
  269.5 2.5 copy-start.1
  273.4 7.6 %copy-start.5 = (bf16[3,256,2048]{2,1,0:T(8,128)(2,1)S(1)}, bf16[3,256,2048]{2,1,0:T(8,128)(2,1)}, u32[]{:S(2)}) copy-start(bf16[3,256,2048]{2,1,0:T(8,128)(2,1)} %param.5) | copy-start | bytes 9437188
  273.4 7.6 %copy-start.18 = (bf16[3,6,2048]{2,1,0:T(8,128)(2,1)S(1)}, bf16[3,6,2048]{2,1,0:T(8,128)(2,1)}, u32[]{:S(2)}) copy-start(bf16[3,6,2048]{2,1,0:T(8,128)(2,1)} %copy-done.17) | copy-start | bytes 221188
  (3 other events, 3.1 us)
Sparse Core Ops, SparseCore 0:
  446.0 54.8 all-reduce.5
where the time goes:
time: 519 us; the launch traced here: 510 us
  local copies, waits for them, and re-layouts  292 us (56%)
  other arithmetic  83.1 us (16%)
  waiting for transfers between devices  53.8 us (10%)
  matrix products  29.8 us (6%)
  blocking collectives  26.5 us (5%)
  between operations  15.1 us (3%)
  starting transfers between devices  9.76 us (2%)
    gather x2, local copies, waits for them, and re-layouts, toeplitz_blocks(): return jnp.take(extra, picks, axis=1)  128 us
    psum x1, waiting for transfers between devices, body(): lax.psum((long_local, skip_local, short_local), 'ctx')  53.8 us
    reshape x1, local copies, waits for them, and re-layouts, diagonal_sums(): folded = flat.reshape(groups, 128, 383).sum(axis=1)  31.9 us
    unnamed x61, local copies, waits for them, and re-layouts  28.5 us
    reshape x1, local copies, waits for them, and re-layouts, diagonal_sums(): flat = jnp.pad(padded.reshape(groups, 128 * 382), ((0, 0), (0, 128)))  26.9 us
    psum x1, blocking collectives, body(): lax.psum((long_local, skip_local, short_local), 'ctx')  26.5 us
    pad x1, local copies, waits for them, and re-layouts, diagonal_sums(): flat = jnp.pad(padded.reshape(groups, 128 * 382), ((0, 0), (0, 128)))  17 us
    pad x1, local copies, waits for them, and re-layouts, diagonal_sums(): padded = jnp.pad(grid, ((0, 0), (0, 0), (0, 126)))  15 us
  transfers between devices with their start and end apart: 4, of which 1 were waited for; matrix products, arithmetic and copies ran while one was open for 37% of the time, Pallas kernels for 0%

commit v1 on v0

v1 whole, which is shorter than its diff:
```python
import functools
import math

import jax
import jax.numpy as jnp
from jax import lax
from jax.experimental import pallas as pl
from jax.experimental.pallas import tpu as pltpu
from jax.sharding import PartitionSpec as P

F32 = jnp.float32
BF16 = jnp.bfloat16
LANES = 128
EDGE = 16
CHUNK = 64
MESH = pl.DeviceIdType.MESH
EXACT = lax.Precision.HIGHEST


def lanes_of(tile):
    return pl.ds(pl.multiple_of(tile * LANES, LANES), LANES)


def spread(row, width):
    wide = jnp.concatenate([row, jnp.zeros_like(row)], axis=1)
    return jnp.broadcast_to(wide, (LANES, width))


def kernel(
    n,
    tiles,
    rows,
    reduce_here,
    feat_ref,
    taps_ref,
    long_ref,
    gain_ref,
    cot_ref,
    gated_ref,
    fgrad_ref,
    red_out,
    edge,
    padf,
    mixed,
    prod,
    gi,
    gm,
    gmf,
    causal,
    ahead,
    flipped,
    red_in,
    red_recv,
    edge_sem,
    tail_sem,
    head_sem,
    gm_sem,
    scatter_sem,
    gather_sem,
):
    me = lax.axis_index("ctx")
    nxt = lax.rem(me + 1, n)
    prv = lax.rem(me + n - 1, n)
    has_prev = me > 0
    has_next = me < n - 1
    groups = 8 * tiles
    units = red_out.shape[0]
    share = units // n if reduce_here else 0

    def remote(src, dst, sems, index, device):
        return pltpu.make_async_remote_copy(
            src_ref=src,
            dst_ref=dst,
            send_sem=sems.at[0, index],
            recv_sem=sems.at[1, index],
            device_id={"ctx": device},
            device_id_type=MESH,
        )

    def edge_copy():
        return remote(feat_ref.at[:, pl.ds(rows - EDGE, EDGE)], edge, edge_sem, 0, nxt)

    def tail_copy(t):
        return remote(
            prod.at[t, pl.ds(rows, LANES)], prod.at[t, pl.ds(0, LANES)], tail_sem, t, nxt
        )

    def head_copy(t):
        return remote(gi.at[t, pl.ds(0, LANES)], gi.at[t, pl.ds(rows, LANES)], head_sem, t, prv)

    def gm_copy(t):
        return remote(
            gm.at[t, :, pl.ds(0, EDGE)], gm.at[t, :, pl.ds(rows, EDGE)], gm_sem, t, prv
        )

    def scatter_copy(k):
        peer = lax.rem(me + k, n)
        return remote(
            red_in.at[pl.ds(peer * share, share)], red_recv.at[k - 1], scatter_sem, k - 1, peer
        )

    def gather_copy(k):
        peer = lax.rem(me + k, n)
        mine = red_out.at[pl.ds(me * share, share)]
        return remote(mine, mine, gather_sem, k - 1, peer)

    barrier = pltpu.get_barrier_semaphore()
    if reduce_here:
        for k in range(1, n):
            pl.semaphore_signal(
                barrier, inc=1, device_id={"ctx": lax.rem(me + k, n)}, device_id_type=MESH
            )
        pl.semaphore_wait(barrier, n - 1)
    else:

        @pl.when(has_prev)
        def _():
            pl.semaphore_signal(barrier, inc=1, device_id={"ctx": prv}, device_id_type=MESH)

        @pl.when(has_next)
        def _():
            pl.semaphore_signal(barrier, inc=1, device_id={"ctx": nxt}, device_id_type=MESH)

        @pl.when(has_prev)
        def _():
            pl.semaphore_wait(barrier, 1)

        @pl.when(has_next)
        def _():
            pl.semaphore_wait(barrier, 1)

    @pl.when(has_next)
    def _():
        edge_copy().start()

    @pl.when(jnp.logical_not(has_prev))
    def _():
        edge[...] = jnp.zeros_like(edge)
        prod[:, :LANES] = jnp.zeros((tiles, LANES, LANES), BF16)

    @pl.when(jnp.logical_not(has_next))
    def _():
        gi[:, rows:] = jnp.zeros((tiles, LANES, LANES), BF16)
        gm[:, :, rows:] = jnp.zeros((tiles, 3, EDGE, LANES), BF16)

    anti = (
        lax.broadcasted_iota(jnp.int32, (LANES, LANES), 0)
        + lax.broadcasted_iota(jnp.int32, (LANES, LANES), 1)
        == LANES - 1
    ).astype(F32)
    anti_b = anti.astype(BF16)
    flipped[...] = jnp.dot(long_ref[...], anti_b, preferred_element_type=F32)

    def build_causal(t, carry):
        part = flipped[pl.ds(pl.multiple_of(t * 8, 8), 8), :]
        for g in range(8):
            causal[t, g] = pltpu.roll(
                spread(part[g : g + 1], 2 * LANES), 1, 1, stride=1, stride_axis=0
            ).astype(BF16)
        return carry

    lax.fori_loop(0, tiles, build_causal, 0)

    @pl.when(has_prev)
    def _():
        edge_copy().wait_recv()

    def front(t, carry):
        cols = lanes_of(t)
        for i in range(3):
            padf[t, i, :EDGE] = edge[i, :, cols].astype(F32)
            padf[t, i, EDGE:] = feat_ref[i, :, cols].astype(F32)
        for start in range(0, rows, CHUNK):
            values = []
            for i in range(3):
                total = jnp.zeros((CHUNK, LANES), F32)
                for j in range(7):
                    total = total + taps_ref[i, pl.ds(j, 1), cols] * padf[
                        t, i, pl.ds(EDGE - j + start, CHUNK)
                    ]
                rounded = total.astype(BF16)
                mixed[t, i, pl.ds(start, CHUNK)] = rounded
                values.append(rounded.astype(F32))
            query, key, value = values
            prod[t, pl.ds(LANES + start, CHUNK)] = (key * value).astype(BF16)
            grad_in = cot_ref[pl.ds(start, CHUNK), cols].astype(F32)
            gi[t, pl.ds(start, CHUNK)] = (grad_in * query).astype(BF16)

        @pl.when(has_next)
        def _():
            tail_copy(t).start()

        @pl.when(has_prev)
        def _():
            head_copy(t).start()

        return carry

    lax.fori_loop(0, tiles, front, 0)

    flipped[...] = long_ref[...].astype(F32)

    def build_ahead(t, carry):
        part = flipped[pl.ds(pl.multiple_of(t * 8, 8), 8), :]
        for g in range(8):
            ahead[t, g] = pltpu.roll(
                spread(part[g : g + 1], 2 * LANES), 0, 1, stride=1, stride_axis=0
            ).astype(BF16)
        return carry

    lax.fori_loop(0, tiles, build_ahead, 0)

    lane_group = lax.rem(
        lax.broadcasted_iota(jnp.int32, (LANES, 2 * LANES), 1), LANES
    ) // 16
    blocks = rows // LANES

    def pair(ref, t, first):
        return jnp.concatenate(
            [ref[t, pl.ds(first, LANES)], ref[t, pl.ds(first + LANES, LANES)]], axis=1
        )

    def middle(t, short_acc):
        cols = lanes_of(t)

        @pl.when(has_prev)
        def _():
            tail_copy(t).wait_recv()

        @pl.when(has_next)
        def _():
            head_copy(t).wait_recv()

        gain = gain_ref[:, cols].astype(F32)
        skip = jnp.zeros((8, LANES), F32)
        folds = [jnp.zeros((1, LANES), F32)] * 8
        for first in range(0, rows, 2 * LANES):
            span = 2 * LANES
            window = jnp.concatenate(
                [prod[t, pl.ds(first, span)], prod[t, pl.ds(first + LANES, span)]], axis=1
            )
            coming = jnp.concatenate(
                [gi[t, pl.ds(first, span)], gi[t, pl.ds(first + LANES, span)]], axis=1
            )
            conv = jnp.zeros((LANES, 2 * LANES), F32)
            back = jnp.zeros((LANES, 2 * LANES), F32)
            turned = jnp.dot(anti_b, pair(gi, t, first), preferred_element_type=F32)
            for g in range(8):
                own = lane_group == g
                one = jnp.dot(causal[t, g], window, preferred_element_type=F32)
                conv = jnp.where(own, one, conv)
                two = jnp.dot(ahead[t, g], coming, preferred_element_type=F32)
                back = jnp.where(own, two, back)
                grid = lax.dot_general(
                    jnp.where(own, turned, 0.0).astype(BF16),
                    window,
                    (((1,), (1,)), ((), ())),
                    preferred_element_type=F32,
                )
                lined = pltpu.roll(grid, 0, 1, stride=1, stride_axis=0)
                folds[g] = folds[g] + jnp.sum(lined[:, LANES:], axis=0, keepdims=True)
            for half in range(2):
                start = first + half * LANES
                here = slice(half * LANES, (half + 1) * LANES)
                at = pl.ds(start, LANES)
                product = prod[t, pl.ds(start + LANES, LANES)].astype(F32)
                grad_inner = gi[t, at].astype(F32)
                query = mixed[t, 0, at].astype(F32)
                key = mixed[t, 1, at].astype(F32)
                value = mixed[t, 2, at].astype(F32)
                inner = conv[:, here] + gain * product
                gated_ref[at, cols] = (query * inner).astype(BF16)
                gm[t, 0, at] = (cot_ref[at, cols].astype(F32) * inner).astype(BF16)
                grad_prod = (back[:, here] + gain * grad_inner).astype(BF16).astype(F32)
                gm[t, 1, at] = (grad_prod * value).astype(BF16)
                gm[t, 2, at] = (grad_prod * key).astype(BF16)
                skip = skip + jnp.sum(
                    (grad_inner * product).reshape(LANES // 8, 8, LANES), axis=0
                )

        @pl.when(has_prev)
        def _():
            gm_copy(t).start()

        red_in[t] = jnp.concatenate(folds, axis=0)
        red_in[tiles + t // 8, pl.ds(lax.rem(t, 8), 1)] = jnp.sum(skip, axis=0, keepdims=True)
        sums = []
        for i in range(3):
            parts = [jnp.zeros((8, LANES), F32)] * 7
            for start in range(0, rows, CHUNK):
                grad = gm[t, i, pl.ds(start, CHUNK)].astype(F32)
                for j in range(7):
                    term = grad * padf[t, i, pl.ds(EDGE - j + start, CHUNK)]
                    parts[j] = parts[j] + jnp.sum(term.reshape(CHUNK // 8, 8, LANES), axis=0)
            sums += [jnp.sum(part, axis=0, keepdims=True) for part in parts]
            sums.append(jnp.zeros((1, LANES), F32))
        member = (
            lax.broadcasted_iota(jnp.int32, (LANES, LANES), 0) // 16 + t * 8
            == lax.broadcasted_iota(jnp.int32, (LANES, LANES), 1)
        ).astype(F32)
        return short_acc + jnp.dot(
            jnp.concatenate(sums, axis=0), member, precision=EXACT, preferred_element_type=F32
        )

    skip_units = (tiles + 7) // 8
    red_in[tiles:] = jnp.zeros((units - tiles, 8, LANES), F32)
    short_sum = lax.fori_loop(0, tiles, middle, jnp.zeros((24, LANES), F32))
    at_short = tiles + skip_units
    red_in[at_short : at_short + 3] = short_sum.reshape(3, 8, LANES)
    lags = red_in[:tiles].reshape(groups, LANES)
    lags = jnp.dot(lags, anti, precision=EXACT, preferred_element_type=F32)
    red_in[:tiles] = lags.reshape(tiles, 8, LANES)
    if reduce_here:
        for k in range(1, n):
            scatter_copy(k).start()
    else:
        red_out[...] = red_in[...]

    def finish(t, carry):
        cols = lanes_of(t)

        @pl.when(has_next)
        def _():
            gm_copy(t).wait_recv()

        for i in range(3):
            gmf[i] = gm[t, i].astype(F32)
        for start in range(0, rows, CHUNK):
            for i in range(3):
                total = jnp.zeros((CHUNK, LANES), F32)
                for j in range(7):
                    total = total + taps_ref[i, pl.ds(j, 1), cols] * gmf[
                        i, pl.ds(start + j, CHUNK)
                    ]
                fgrad_ref[i, pl.ds(start, CHUNK), cols] = total.astype(BF16)
        return carry

    if reduce_here:
        half = tiles // 2
        lax.fori_loop(0, half, finish, 0)
        total = red_in[pl.ds(me * share, share)]
        for k in range(1, n):
            scatter_copy(k).wait_recv()
            total = total + red_recv[k - 1]
        red_out[pl.ds(me * share, share)] = total
        for k in range(1, n):
            gather_copy(k).start()
        lax.fori_loop(half, tiles, finish, 0)
    else:
        lax.fori_loop(0, tiles, finish, 0)

    @pl.when(has_next)
    def _():
        edge_copy().wait_send()

    def drain(t, carry):
        @pl.when(has_next)
        def _():
            tail_copy(t).wait_send()

        @pl.when(has_prev)
        def _():
            head_copy(t).wait_send()
            gm_copy(t).wait_send()

        return carry

    lax.fori_loop(0, tiles, drain, 0)
    if reduce_here:
        for k in range(1, n):
            scatter_copy(k).wait_send()
            gather_copy(k).wait()


def body(features, short_taps, long_taps, skip_gain, cotangent):
    rows, width = features.shape[1:]
    tiles = width // LANES
    groups = width // 16
    n = lax.axis_size("ctx")
    skip_units = (tiles + 7) // 8
    units = tiles + skip_units + 3
    reduce_here = n <= 16
    if reduce_here:
        units = -(-units // n) * n
    share = units // n if reduce_here else 1
    peers = n - 1 if reduce_here else 1
    taps = jnp.repeat(jnp.transpose(short_taps, (0, 2, 1)).astype(F32), 16, axis=2)
    vmem = pl.BlockSpec(memory_space=pltpu.VMEM)
    gated, fgrad, red = pl.pallas_call(
        functools.partial(kernel, n, tiles, rows, reduce_here),
        out_shape=(
            jax.ShapeDtypeStruct((rows, width), BF16),
            jax.ShapeDtypeStruct((3, rows, width), BF16),
            jax.ShapeDtypeStruct((units, 8, LANES), F32),
        ),
        in_specs=[vmem] * 5,
        out_specs=(vmem, vmem, vmem),
        scratch_shapes=[
            pltpu.VMEM((3, EDGE, width), BF16),
            pltpu.VMEM((tiles, 3, EDGE + rows, LANES), F32),
            pltpu.VMEM((tiles, 3, rows, LANES), BF16),
            pltpu.VMEM((tiles, LANES + rows, LANES), BF16),
            pltpu.VMEM((tiles, rows + LANES, LANES), BF16),
            pltpu.VMEM((tiles, 3, rows + EDGE, LANES), BF16),
            pltpu.VMEM((3, rows + EDGE, LANES), F32),
            pltpu.VMEM((tiles, 8, LANES, 2 * LANES), BF16),
            pltpu.VMEM((tiles, 8, LANES, 2 * LANES), BF16),
            pltpu.VMEM((groups, LANES), F32),
            pltpu.VMEM((units, 8, LANES), F32),
            pltpu.VMEM((peers, share, 8, LANES), F32),
            pltpu.SemaphoreType.DMA((2, 1)),
            pltpu.SemaphoreType.DMA((2, tiles)),
            pltpu.SemaphoreType.DMA((2, tiles)),
            pltpu.SemaphoreType.DMA((2, tiles)),
            pltpu.SemaphoreType.DMA((2, peers)),
            pltpu.SemaphoreType.DMA((2, peers)),
        ],
        compiler_params=pltpu.CompilerParams(
            collective_id=0, has_side_effects=True, vmem_limit_bytes=60 * 1024 * 1024
        ),
        cost_estimate=pl.CostEstimate(
            flops=12 * rows * width * LANES * 8, bytes_accessed=16 * rows * width, transcendentals=0
        ),
    )(features, taps, long_taps, skip_gain.reshape(1, width), cotangent)
    if not reduce_here:
        red = lax.psum(red, "ctx")
    total = rows * n
    group_scale = 1.0 / math.sqrt(16.0 * total)
    token_scale = 1.0 / math.sqrt(1.0 * total)
    long_grad = red[:tiles].reshape(groups, LANES) * group_scale
    skip_grad = red[tiles : tiles + skip_units].reshape(-1)[:width] * token_scale
    short = red[tiles + skip_units : tiles + skip_units + 3]
    short_grad = jnp.transpose(short[:, :7, :groups], (0, 2, 1)) * group_scale
    return gated, fgrad, short_grad, long_grad, skip_grad


def solution(mesh):
    placed = (P(None, "ctx", "tp"), P(None, "tp", None), P("tp", None), P("tp"), P("ctx", "tp"))
    return jax.shard_map(
        body,
        mesh=mesh,
        in_specs=placed,
        out_specs=(
            P("ctx", "tp"),
            P(None, "ctx", "tp"),
            P(None, "tp", None),
            P("tp", None),
            P("tp"),
        ),
        check_vma=False,
    )
```

time: 519 us -> 64.5 us (0.12); the launches traced: 510 us -> 64.1 us
  local copies, waits for them, and re-layouts: 292 us -> 9.44 us
  other arithmetic: 83.1 us -> 4.78 us
  waiting for transfers between devices: 53.8 us -> 0 us
  Pallas kernels: 0 us -> 49.2 us
  matrix products: 29.8 us -> 0 us
  blocking collectives: 26.5 us -> 0 us
  between operations: 15.1 us -> 0.65 us
  starting transfers between devices: 9.76 us -> 0 us
    gather x4 -> x0, local copies, waits for them, and re-layouts: 137 us -> none  [the longest x2 128 us: toeplitz_blocks(): return jnp.take(extra, picks, axis=1)]
    reshape x10 -> x2, local copies, waits for them, and re-layouts: 77.7 us -> 2.75 us  [the longest x1 1.46 us: body(): jnp.repeat(jnp.transpose(short_taps, (0, 2, 1)).astype(F32), 16, axis=2)]
    psum x1 -> x0, waiting for transfers between devices: 53.8 us -> none  [body(): lax.psum((long_local, skip_local, short_local), 'ctx')]
    pallas_call x0 -> x1, Pallas kernels: none -> 49.2 us  [body(): pl.pallas_call(functools.partial(kernel, n, tiles, rows, reduce_here), ou...]
    pad x2 -> x0, local copies, waits for them, and re-layouts: 32 us -> none  [the longest x1 17 us: diagonal_sums(): flat = jnp.pad(padded.reshape(groups, 128 * 382), ((0, 0), (0, 128)))]
    dot_general x6 -> x0, matrix products: 29.8 us -> none  [the longest x1 5.87 us: body(): jnp.einsum('gts,gns->gnt', earlier, before, preferred_element_type=jnp.fl...]
    psum x1 -> x0, blocking collectives: 26.5 us -> none  [body(): lax.psum((long_local, skip_local, short_local), 'ctx')]
    unnamed x61 -> x2, local copies, waits for them, and re-layouts: 28.5 us -> 6.27 us
  transfers between devices with their start and end apart: 4 -> 0, of which waited for: 1 -> 0; matrix products, arithmetic and copies ran while one was open for 37% -> 0% of each run, Pallas kernels for 0% -> 0%
where the time goes in v1:
time: 64.5 us; the launch traced here: 64.1 us
  Pallas kernels  49.2 us (76%)
  local copies, waits for them, and re-layouts  9.44 us (15%)
  other arithmetic  4.78 us (7%)
  between operations  0.65 us (1%)
    pallas_call x1, Pallas kernels, body(): pl.pallas_call(functools.partial(kernel, n, tiles, rows, reduce_here), ou...  49.2 us
    unnamed x2, local copies, waits for them, and re-layouts  6.27 us
    mul x1, other arithmetic, body(): long_grad = red[:tiles].reshape(groups, LANES) * group_scale  1.47 us
    reshape x1, local copies, waits for them, and re-layouts, body(): jnp.repeat(jnp.transpose(short_taps, (0, 2, 1)).astype(F32), 16, axis=2)  1.46 us
    mul x1, other arithmetic, body(): short_grad = jnp.transpose(short[:, :7, :groups], (0, 2, 1)) * group_scale  1.31 us
    mul x1, other arithmetic, body(): skip_grad = red[tiles:tiles + skip_units].reshape(-1)[:width] * token_scale  1.3 us
    reshape x1, local copies, waits for them, and re-layouts, body(): skip_gain.reshape(1, width)  1.29 us

profile of v1, /device:TPU:0, one launch (start us, length us, event | category | flops | bytes accessed | tf_op | source)
XLA Modules:
  0.0 64.1 jit_solution(2539876294492950731)
XLA Ops:
  0.6 1.3 %reshape.23.gain_ref = bf16[1,2048]{1,0:T(2,128)(2,1)} reshape(bf16[2048]{0:T(1024)(128)(2,1)} %param.8) | data formatting | bytes 8192 | tf_op jit(solution)/shard_map/reshape | solution.py:424
  1.9 0.7 %convert_bitcast_fusion = f32[3,7,128]{2,1,0:T(8,128)S(1)} fusion(bf16[3,128,7]{1,2,0:T(8,128)(2,1)} %param.6), kind=kLoop, calls=%fused_computation.1 | loop fusion | flops 2688 | bytes 16128 | tf_op jit(solution)/shard_map/convert_element_type | solution.py:387
  2.6 0.4 broadcast_in_dim.3
  3.0 1.5 %reshape.22.taps_ref = f32[3,7,2048]{2,1,0:T(8,128)} reshape(f32[3,7,128,16]{3,2,1,0:T(8,128)S(1)} %broadcast_in_dim.3) | data formatting | bytes 344064 | tf_op jit(solution)/shard_map/reshape | solution.py:387
  4.5 49.2 %shard_map.92 = (bf16[256,2048]{1,0:T(8,128)(2,1)}, bf16[3,256,2048]{2,1,0:T(8,128)(2,1)}, f32[24,8,128]{2,1,0:T(8,128)}) custom-call(bf16[3,256,2048]{2,1,0:T(8,128)(2,1)} %feat_ref.1, f32[3,7,2048]{2,1,0:T(8,128)} %reshape.22.taps_ref, bf16[128,128]{1,0:T(8,128)(2,1)} %long_ref.1, bf16[1,2048]{1,0:T(2,128)(2,1)} %reshape.23.gain_ref, bf16[256,2048]{1,0:T(8,128)(2,1)} %cot_ref.1), custom_call_target="tpu_custom_call" | custom-call | flops 6442450944 | bytes 8388608 | tf_op jit(solution)/shard_map/pallas_call | solution.py:389
  53.7 1.3 %multiply_bitcast_fusion.2 = f32[2048]{0:T(1024)} fusion(f32[24,8,128]{2,1,0:T(8,128)} %get-tuple-element.10), kind=kLoop, calls=%fused_computation.3 | loop fusion | flops 2048 | bytes 16384 | tf_op jit(solution)/shard_map/mul | solution.py:431
  55.0 1.3 %multiply_bitcast_fusion.1 = f32[3,128,7]{1,2,0:T(8,128)} fusion(f32[24,8,128]{2,1,0:T(8,128)} %get-tuple-element.10), kind=kLoop, calls=%fused_computation.2 | loop fusion | flops 2688 | bytes 21504 | tf_op jit(solution)/shard_map/mul | solution.py:433
  56.3 1.5 %multiply_bitcast_fusion = f32[128,128]{1,0:T(8,128)} fusion(f32[24,8,128]{2,1,0:T(8,128)} %get-tuple-element.10), kind=kLoop, calls=%fused_computation | loop fusion | flops 16384 | bytes 131072 | tf_op jit(solution)/shard_map/mul | solution.py:430
  57.8 2.3 %copy.12 = bf16[256,2048]{1,0:T(8,128)(2,1)} copy(bf16[256,2048]{1,0:T(8,128)(2,1)} %get-tuple-element.16) | data formatting | bytes 2097152
  60.1 4.0 %copy.13 = bf16[3,256,2048]{2,1,0:T(8,128)(2,1)} copy(bf16[3,256,2048]{2,1,0:T(8,128)(2,1)} %get-tuple-element.17) | data formatting | bytes 6291456

commit v2 on v1

--- a/solution.py
+++ b/solution.py
@@ -21,9 +21,19 @@
     return pl.ds(pl.multiple_of(tile * LANES, LANES), LANES)
 
 
-def spread(row, width):
-    wide = jnp.concatenate([row, jnp.zeros_like(row)], axis=1)
-    return jnp.broadcast_to(wide, (LANES, width))
+def tile_taps(taps_ref, tile):
+    groups = taps_ref.shape[2]
+    member = (
+        lax.broadcasted_iota(jnp.int32, (groups, LANES), 0)
+        == lax.broadcasted_iota(jnp.int32, (groups, LANES), 1) // 16 + tile * 8
+    ).astype(F32).astype(BF16)
+    return [jnp.dot(taps_ref[i], member, preferred_element_type=F32) for i in range(3)]
+
+
+def circulant(row, shift):
+    return pltpu.roll(
+        jnp.broadcast_to(row, (LANES, LANES)), shift, 1, stride=1, stride_axis=0
+    )
 
 
 def kernel(
@@ -37,18 +47,17 @@
     gain_ref,
     cot_ref,
     gated_ref,
-    fgrad_ref,
+    gm,
     red_out,
     edge,
     padf,
     mixed,
     prod,
     gi,
-    gm,
-    gmf,
     causal,
     ahead,
     flipped,
+    gainf,
     red_in,
     red_recv,
     edge_sem,
@@ -143,20 +152,21 @@
         gi[:, rows:] = jnp.zeros((tiles, LANES, LANES), BF16)
         gm[:, :, rows:] = jnp.zeros((tiles, 3, EDGE, LANES), BF16)
 
-    anti = (
-        lax.broadcasted_iota(jnp.int32, (LANES, LANES), 0)
-        + lax.broadcasted_iota(jnp.int32, (LANES, LANES), 1)
-        == LANES - 1
-    ).astype(F32)
+    row_pos = lax.broadcasted_iota(jnp.int32, (LANES, LANES), 0)
+    col_pos = lax.broadcasted_iota(jnp.int32, (LANES, LANES), 1)
+    above = col_pos > row_pos
+    below = col_pos < row_pos
+    past = col_pos + row_pos > LANES - 1
+    anti = (row_pos + col_pos == LANES - 1).astype(F32)
     anti_b = anti.astype(BF16)
     flipped[...] = jnp.dot(long_ref[...], anti_b, preferred_element_type=F32)
 
     def build_causal(t, carry):
         part = flipped[pl.ds(pl.multiple_of(t * 8, 8), 8), :]
         for g in range(8):
-            causal[t, g] = pltpu.roll(
-                spread(part[g : g + 1], 2 * LANES), 1, 1, stride=1, stride_axis=0
-            ).astype(BF16)
+            turned = circulant(part[g : g + 1], 1)
+            causal[t, g, :, :LANES] = jnp.where(above, turned, 0.0).astype(BF16)
+            causal[t, g, :, LANES:] = jnp.where(above, 0.0, turned).astype(BF16)
         return carry
 
     lax.fori_loop(0, tiles, build_causal, 0)
@@ -165,8 +175,11 @@
     def _():
         edge_copy().wait_recv()
 
+    gainf[...] = gain_ref[...].astype(F32)
+
     def front(t, carry):
         cols = lanes_of(t)
+        taps = tile_taps(taps_ref, t)
         for i in range(3):
             padf[t, i, :EDGE] = edge[i, :, cols].astype(F32)
             padf[t, i, EDGE:] = feat_ref[i, :, cols].astype(F32)
@@ -175,7 +188,7 @@
             for i in range(3):
                 total = jnp.zeros((CHUNK, LANES), F32)
                 for j in range(7):
-                    total = total + taps_ref[i, pl.ds(j, 1), cols] * padf[
+                    total = total + taps[i][j : j + 1] * padf[
                         t, i, pl.ds(EDGE - j + start, CHUNK)
                     ]
                 rounded = total.astype(BF16)
@@ -203,9 +216,9 @@
     def build_ahead(t, carry):
         part = flipped[pl.ds(pl.multiple_of(t * 8, 8), 8), :]
         for g in range(8):
-            ahead[t, g] = pltpu.roll(
-                spread(part[g : g + 1], 2 * LANES), 0, 1, stride=1, stride_axis=0
-            ).astype(BF16)
+            turned = circulant(part[g : g + 1], 0)
+            ahead[t, g, :, :LANES] = jnp.where(below, 0.0, turned).astype(BF16)
+            ahead[t, g, :, LANES:] = jnp.where(below, turned, 0.0).astype(BF16)
         return carry
 
     lax.fori_loop(0, tiles, build_ahead, 0)
@@ -231,7 +244,7 @@
         def _():
             head_copy(t).wait_recv()
 
-        gain = gain_ref[:, cols].astype(F32)
+        gain = gainf[pl.ds(t, 1)]
         skip = jnp.zeros((8, LANES), F32)
         folds = [jnp.zeros((1, LANES), F32)] * 8
         for first in range(0, rows, 2 * LANES):
@@ -257,8 +270,9 @@
                     (((1,), (1,)), ((), ())),
                     preferred_element_type=F32,
                 )
-                lined = pltpu.roll(grid, 0, 1, stride=1, stride_axis=0)
-                folds[g] = folds[g] + jnp.sum(lined[:, LANES:], axis=0, keepdims=True)
+                ring = jnp.where(past, grid[:, :LANES], grid[:, LANES:])
+                lined = pltpu.roll(ring, 0, 1, stride=1, stride_axis=0)
+                folds[g] = folds[g] + jnp.sum(lined, axis=0, keepdims=True)
             for half in range(2):
                 start = first + half * LANES
                 here = slice(half * LANES, (half + 1) * LANES)
@@ -269,7 +283,7 @@
                 key = mixed[t, 1, at].astype(F32)
                 value = mixed[t, 2, at].astype(F32)
                 inner = conv[:, here] + gain * product
-                gated_ref[at, cols] = (query * inner).astype(BF16)
+                gated_ref[t, at] = (query * inner).astype(BF16)
                 gm[t, 0, at] = (cot_ref[at, cols].astype(F32) * inner).astype(BF16)
                 grad_prod = (back[:, here] + gain * grad_inner).astype(BF16).astype(F32)
                 gm[t, 1, at] = (grad_prod * value).astype(BF16)
@@ -316,28 +330,7 @@
     else:
         red_out[...] = red_in[...]
 
-    def finish(t, carry):
-        cols = lanes_of(t)
-
-        @pl.when(has_next)
-        def _():
-            gm_copy(t).wait_recv()
-
-        for i in range(3):
-            gmf[i] = gm[t, i].astype(F32)
-        for start in range(0, rows, CHUNK):
-            for i in range(3):
-                total = jnp.zeros((CHUNK, LANES), F32)
-                for j in range(7):
-                    total = total + taps_ref[i, pl.ds(j, 1), cols] * gmf[
-                        i, pl.ds(start + j, CHUNK)
-                    ]
-                fgrad_ref[i, pl.ds(start, CHUNK), cols] = total.astype(BF16)
-        return carry
-
     if reduce_here:
-        half = tiles // 2
-        lax.fori_loop(0, half, finish, 0)
         total = red_in[pl.ds(me * share, share)]
         for k in range(1, n):
             scatter_copy(k).wait_recv()
@@ -345,9 +338,6 @@
         red_out[pl.ds(me * share, share)] = total
         for k in range(1, n):
             gather_copy(k).start()
-        lax.fori_loop(half, tiles, finish, 0)
-    else:
-        lax.fori_loop(0, tiles, finish, 0)
 
     @pl.when(has_next)
     def _():
@@ -357,6 +347,7 @@
         @pl.when(has_next)
         def _():
             tail_copy(t).wait_send()
+            gm_copy(t).wait_recv()
 
         @pl.when(has_prev)
         def _():
@@ -370,6 +361,49 @@
         for k in range(1, n):
             scatter_copy(k).wait_send()
             gather_copy(k).wait()
+
+
+def finish(
+    step_tiles,
+    rows,
+    group_scale,
+    token_scale,
+    gated_in,
+    gm,
+    red,
+    taps_ref,
+    gated_ref,
+    fgrad_ref,
+    long_ref,
+    skip_ref,
+    short_ref,
+    gmf,
+):
+    groups = long_ref.shape[0]
+    tiles = groups // 8
+    skip_units = skip_ref.shape[0] // 8
+
+    @pl.when(pl.program_id(0) == 0)
+    def _():
+        long_ref[...] = red[:tiles].reshape(groups, LANES) * group_scale
+        skip_ref[...] = red[tiles : tiles + skip_units].reshape(skip_units * 8, LANES) * token_scale
+        for i in range(3):
+            short_ref[i] = red[tiles + skip_units + i][:7, :groups] * group_scale
+
+    for u in range(step_tiles):
+        cols = pl.ds(u * LANES, LANES)
+        taps = tile_taps(taps_ref, pl.program_id(0) * step_tiles + u)
+        gated_ref[:, cols] = gated_in[u]
+        for i in range(3):
+            gmf[i] = gm[u, i].astype(F32)
+        for start in range(0, rows, CHUNK):
+            for i in range(3):
+                total = jnp.zeros((CHUNK, LANES), F32)
+                for j in range(7):
+                    total = total + taps[i][j : j + 1] * gmf[
+                        i, pl.ds(start + j, CHUNK)
+                    ]
+                fgrad_ref[i, pl.ds(start, CHUNK), cols] = total.astype(BF16)
 
 
 def body(features, short_taps, long_taps, skip_gain, cotangent):
@@ -384,13 +418,13 @@
         units = -(-units // n) * n
     share = units // n if reduce_here else 1
     peers = n - 1 if reduce_here else 1
-    taps = jnp.repeat(jnp.transpose(short_taps, (0, 2, 1)).astype(F32), 16, axis=2)
+    taps = jnp.transpose(short_taps, (0, 2, 1))
     vmem = pl.BlockSpec(memory_space=pltpu.VMEM)
-    gated, fgrad, red = pl.pallas_call(
+    gated, grad_mixed, red = pl.pallas_call(
         functools.partial(kernel, n, tiles, rows, reduce_here),
         out_shape=(
-            jax.ShapeDtypeStruct((rows, width), BF16),
-            jax.ShapeDtypeStruct((3, rows, width), BF16),
+            jax.ShapeDtypeStruct((tiles, rows, LANES), BF16),
+            jax.ShapeDtypeStruct((tiles, 3, rows + EDGE, LANES), BF16),
             jax.ShapeDtypeStruct((units, 8, LANES), F32),
         ),
         in_specs=[vmem] * 5,
@@ -401,11 +435,10 @@
             pltpu.VMEM((tiles, 3, rows, LANES), BF16),
             pltpu.VMEM((tiles, LANES + rows, LANES), BF16),
             pltpu.VMEM((tiles, rows + LANES, LANES), BF16),
-            pltpu.VMEM((tiles, 3, rows + EDGE, LANES), BF16),
-            pltpu.VMEM((3, rows + EDGE, LANES), F32),
             pltpu.VMEM((tiles, 8, LANES, 2 * LANES), BF16),
             pltpu.VMEM((tiles, 8, LANES, 2 * LANES), BF16),
             pltpu.VMEM((groups, LANES), F32),
+            pltpu.VMEM((tiles, LANES), F32),
             pltpu.VMEM((units, 8, LANES), F32),
             pltpu.VMEM((peers, share, 8, LANES), F32),
             pltpu.SemaphoreType.DMA((2, 1)),
@@ -421,17 +454,42 @@
         cost_estimate=pl.CostEstimate(
             flops=12 * rows * width * LANES * 8, bytes_accessed=16 * rows * width, transcendentals=0
         ),
-    )(features, taps, long_taps, skip_gain.reshape(1, width), cotangent)
+    )(features, taps, long_taps, skip_gain.reshape(tiles, LANES), cotangent)
     if not reduce_here:
         red = lax.psum(red, "ctx")
     total = rows * n
     group_scale = 1.0 / math.sqrt(16.0 * total)
     token_scale = 1.0 / math.sqrt(1.0 * total)
-    long_grad = red[:tiles].reshape(groups, LANES) * group_scale
-    skip_grad = red[tiles : tiles + skip_units].reshape(-1)[:width] * token_scale
-    short = red[tiles + skip_units : tiles + skip_units + 3]
-    short_grad = jnp.transpose(short[:, :7, :groups], (0, 2, 1)) * group_scale
-    return gated, fgrad, short_grad, long_grad, skip_grad
+    step_tiles = math.gcd(tiles, 4)
+    span = step_tiles * LANES
+    gated, fgrad, long_grad, skip_grad, short_grad = pl.pallas_call(
+        functools.partial(finish, step_tiles, rows, group_scale, token_scale),
+        grid=(tiles // step_tiles,),
+        out_shape=(
+            jax.ShapeDtypeStruct((rows, width), BF16),
+            jax.ShapeDtypeStruct((3, rows, width), BF16),
+            jax.ShapeDtypeStruct((groups, LANES), F32),
+            jax.ShapeDtypeStruct((skip_units * 8, LANES), F32),
+            jax.ShapeDtypeStruct((3, 7, groups), F32),
+        ),
+        in_specs=[
+            pl.BlockSpec((step_tiles, rows, LANES), lambda t: (t, 0, 0)),
+            pl.BlockSpec((step_tiles, 3, rows + EDGE, LANES), lambda t: (t, 0, 0, 0)),
+            pl.BlockSpec((units, 8, LANES), lambda t: (0, 0, 0)),
+            pl.BlockSpec((3, 7, groups), lambda t: (0, 0, 0)),
+        ],
+        out_specs=(
+            pl.BlockSpec((rows, span), lambda t: (0, t)),
+            pl.BlockSpec((3, rows, span), lambda t: (0, 0, t)),
+            pl.BlockSpec((groups, LANES), lambda t: (0, 0)),
+            pl.BlockSpec((skip_units * 8, LANES), lambda t: (0, 0)),
+            pl.BlockSpec((3, 7, groups), lambda t: (0, 0, 0)),
+        ),
+        scratch_shapes=[pltpu.VMEM((3, rows + EDGE, LANES), F32)],
+        compiler_params=pltpu.CompilerParams(vmem_limit_bytes=60 * 1024 * 1024),
+    )(gated, grad_mixed, red, taps)
+    short_grad = jnp.transpose(short_grad, (0, 2, 1))
+    return gated, fgrad, short_grad, long_grad, skip_grad.reshape(-1)[:width]
 
 
 def solution(mesh):

time: 64.5 us -> 59.5 us (0.922)
  Pallas kernels: 49.2 us -> 58.7 us
  local copies, waits for them, and re-layouts: 9.44 us -> 0 us
  other arithmetic: 4.78 us -> 0 us
    pallas_call x0 -> x1, Pallas kernels: none -> 6.8 us  [body(): pl.pallas_call(functools.partial(finish, step_tiles, rows, group_scale, t...]
    unnamed x2 -> x0, local copies, waits for them, and re-layouts: 6.27 us -> none
    mul x3 -> x0, other arithmetic: 4.08 us -> none  [the longest x1 1.47 us: body(): long_grad = red[:tiles].reshape(groups, LANES) * group_scale]
    reshape x2 -> x0, local copies, waits for them, and re-layouts: 2.75 us -> none  [the longest x1 1.46 us: body(): jnp.repeat(jnp.transpose(short_taps, (0, 2, 1)).astype(F32), 16, axis=2)]
    pallas_call x1, Pallas kernels: 49.2 us -> 51.8 us  [body(): pl.pallas_call(functools.partial(kernel, n, tiles, rows, reduce_here), ou...]
    convert_element_type x1 -> x0, other arithmetic: 0.69 us -> none  [body(): jnp.transpose(short_taps, (0, 2, 1)).astype(F32)]
where the time goes in v2:
time: 59.5 us; the launch traced here: 59.3 us
  Pallas kernels  58.7 us (99%)
  between operations  0.64 us (1%)
    pallas_call x1, Pallas kernels, body(): pl.pallas_call(functools.partial(kernel, n, tiles, rows, reduce_here), ou...  51.8 us
    pallas_call x1, Pallas kernels, body(): pl.pallas_call(functools.partial(finish, step_tiles, rows, group_scale, t...  6.8 us

profile of v2, /device:TPU:0, one launch (start us, length us, event | category | flops | bytes accessed | tf_op | source)
XLA Modules:
  0.0 59.3 jit_solution(689489743002209777)
XLA Ops:
  0.6 51.8 %shard_map.92 = (bf16[16,256,128]{2,1,0:T(8,128)(2,1)}, bf16[16,3,272,128]{3,2,1,0:T(8,128)(2,1)}, f32[24,8,128]{2,1,0:T(8,128)}) custom-call(bf16[3,256,2048]{2,1,0:T(8,128)(2,1)} %feat_ref.1, bf16[3,7,128]{2,1,0:T(8,128)(2,1)} %bitcast.4, bf16[128,128]{1,0:T(8,128)(2,1)} %long_ref.1, bf16[16,128]{1,0:T(8,128)(2,1)} %bitcast.8, bf16[256,2048]{1,0:T(8,128)(2,1)} %cot_ref.1), custom_call_target="tpu_custom_call" | custom-call | flops 6442450944 | bytes 8388608 | tf_op jit(solution)/shard_map/pallas_call | solution.py:423
  52.5 6.8 %shard_map.93 = (bf16[256,2048]{1,0:T(8,128)(2,1)}, bf16[3,256,2048]{2,1,0:T(8,128)(2,1)}, f32[128,128]{1,0:T(8,128)}, f32[16,128]{1,0:T(8,128)}, f32[3,7,128]{2,1,0:T(8,128)}) custom-call(bf16[16,256,128]{2,1,0:T(8,128)(2,1)} %get-tuple-element.13.gated_in, bf16[16,3,272,128]{3,2,1,0:T(8,128)(2,1)} %get-tuple-element.14.gm, ...), custom_call_target="tpu_custom_call" | custom-call | tf_op jit(solution)/shard_map/pallas_call | solution.py:465

commit v3 on v2

--- a/solution.py
+++ b/solution.py
@@ -21,13 +21,14 @@
     return pl.ds(pl.multiple_of(tile * LANES, LANES), LANES)
 
 
-def tile_taps(taps_ref, tile):
+def tile_taps(taps_ref, tile, out):
     groups = taps_ref.shape[2]
     member = (
         lax.broadcasted_iota(jnp.int32, (groups, LANES), 0)
         == lax.broadcasted_iota(jnp.int32, (groups, LANES), 1) // 16 + tile * 8
     ).astype(F32).astype(BF16)
-    return [jnp.dot(taps_ref[i], member, preferred_element_type=F32) for i in range(3)]
+    for i in range(3):
+        out[i, :7] = jnp.dot(taps_ref[i], member, preferred_element_type=F32)
 
 
 def circulant(row, shift):
@@ -58,6 +59,7 @@
     ahead,
     flipped,
     gainf,
+    taps,
     red_in,
     red_recv,
     edge_sem,
@@ -179,7 +181,7 @@
 
     def front(t, carry):
         cols = lanes_of(t)
-        taps = tile_taps(taps_ref, t)
+        tile_taps(taps_ref, t, taps)
         for i in range(3):
             padf[t, i, :EDGE] = edge[i, :, cols].astype(F32)
             padf[t, i, EDGE:] = feat_ref[i, :, cols].astype(F32)
@@ -188,7 +190,7 @@
             for i in range(3):
                 total = jnp.zeros((CHUNK, LANES), F32)
                 for j in range(7):
-                    total = total + taps[i][j : j + 1] * padf[
+                    total = total + taps[i, pl.ds(j, 1)] * padf[
                         t, i, pl.ds(EDGE - j + start, CHUNK)
                     ]
                 rounded = total.astype(BF16)
@@ -258,18 +260,25 @@
             conv = jnp.zeros((LANES, 2 * LANES), F32)
             back = jnp.zeros((LANES, 2 * LANES), F32)
             turned = jnp.dot(anti_b, pair(gi, t, first), preferred_element_type=F32)
+            ones = jnp.dot(
+                causal[t].reshape(8 * LANES, span), window, preferred_element_type=F32
+            )
             for g in range(8):
-                own = lane_group == g
-                one = jnp.dot(causal[t, g], window, preferred_element_type=F32)
-                conv = jnp.where(own, one, conv)
-                two = jnp.dot(ahead[t, g], coming, preferred_element_type=F32)
-                back = jnp.where(own, two, back)
-                grid = lax.dot_general(
-                    jnp.where(own, turned, 0.0).astype(BF16),
-                    window,
-                    (((1,), (1,)), ((), ())),
-                    preferred_element_type=F32,
-                )
+                conv = jnp.where(lane_group == g, ones[g * LANES : (g + 1) * LANES], conv)
+            twos = jnp.dot(
+                ahead[t].reshape(8 * LANES, span), coming, preferred_element_type=F32
+            )
+            for g in range(8):
+                back = jnp.where(lane_group == g, twos[g * LANES : (g + 1) * LANES], back)
+            apart = [jnp.where(lane_group == g, turned, 0.0).astype(BF16) for g in range(8)]
+            grids = lax.dot_general(
+                jnp.concatenate(apart, axis=0),
+                window,
+                (((1,), (1,)), ((), ())),
+                preferred_element_type=F32,
+            )
+            for g in range(8):
+                grid = grids[g * LANES : (g + 1) * LANES]
                 ring = jnp.where(past, grid[:, :LANES], grid[:, LANES:])
                 lined = pltpu.roll(ring, 0, 1, stride=1, stride_axis=0)
                 folds[g] = folds[g] + jnp.sum(lined, axis=0, keepdims=True)
@@ -378,6 +387,7 @@
     skip_ref,
     short_ref,
     gmf,
+    taps,
 ):
     groups = long_ref.shape[0]
     tiles = groups // 8
@@ -392,7 +402,7 @@
 
     for u in range(step_tiles):
         cols = pl.ds(u * LANES, LANES)
-        taps = tile_taps(taps_ref, pl.program_id(0) * step_tiles + u)
+        tile_taps(taps_ref, pl.program_id(0) * step_tiles + u, taps)
         gated_ref[:, cols] = gated_in[u]
         for i in range(3):
             gmf[i] = gm[u, i].astype(F32)
@@ -400,7 +410,7 @@
             for i in range(3):
                 total = jnp.zeros((CHUNK, LANES), F32)
                 for j in range(7):
-                    total = total + taps[i][j : j + 1] * gmf[
+                    total = total + taps[i, pl.ds(j, 1)] * gmf[
                         i, pl.ds(start + j, CHUNK)
                     ]
                 fgrad_ref[i, pl.ds(start, CHUNK), cols] = total.astype(BF16)
@@ -439,6 +449,7 @@
             pltpu.VMEM((tiles, 8, LANES, 2 * LANES), BF16),
             pltpu.VMEM((groups, LANES), F32),
             pltpu.VMEM((tiles, LANES), F32),
+            pltpu.VMEM((3, 8, LANES), F32),
             pltpu.VMEM((units, 8, LANES), F32),
             pltpu.VMEM((peers, share, 8, LANES), F32),
             pltpu.SemaphoreType.DMA((2, 1)),
@@ -485,7 +496,10 @@
             pl.BlockSpec((skip_units * 8, LANES), lambda t: (0, 0)),
             pl.BlockSpec((3, 7, groups), lambda t: (0, 0, 0)),
         ),
-        scratch_shapes=[pltpu.VMEM((3, rows + EDGE, LANES), F32)],
+        scratch_shapes=[
+            pltpu.VMEM((3, rows + EDGE, LANES), F32),
+            pltpu.VMEM((3, 8, LANES), F32),
+        ],
         compiler_params=pltpu.CompilerParams(vmem_limit_bytes=60 * 1024 * 1024),
     )(gated, grad_mixed, red, taps)
     short_grad = jnp.transpose(short_grad, (0, 2, 1))

time: 59.5 us -> 56.4 us (0.948)
  Pallas kernels: 58.7 us -> 55.6 us
    pallas_call x1, Pallas kernels: 51.8 us -> 47.7 us  [body(): pl.pallas_call(functools.partial(kernel, n, tiles, rows, reduce_here), ou...]
    pallas_call x1, Pallas kernels: 6.8 us -> 7.83 us  [body(): pl.pallas_call(functools.partial(finish, step_tiles, rows, group_scale, t...]
where the time goes in v3:
time: 56.4 us; the launch traced here: 56.2 us
  Pallas kernels  55.6 us (99%)
  between operations  0.64 us (1%)
    pallas_call x1, Pallas kernels, body(): pl.pallas_call(functools.partial(kernel, n, tiles, rows, reduce_here), ou...  47.7 us
    pallas_call x1, Pallas kernels, body(): pl.pallas_call(functools.partial(finish, step_tiles, rows, group_scale, t...  7.83 us

profile of v3, /device:TPU:0, one launch (start us, length us, event | category | flops | bytes accessed | tf_op | source)
XLA Modules:
  0.0 56.2 jit_solution(1459988341847136321)
XLA Ops:
  0.6 47.7 %shard_map.92 = (bf16[16,256,128]{2,1,0:T(8,128)(2,1)}, bf16[16,3,272,128]{3,2,1,0:T(8,128)(2,1)}, f32[24,8,128]{2,1,0:T(8,128)}) custom-call(bf16[3,256,2048]{2,1,0:T(8,128)(2,1)} %feat_ref.1, bf16[3,7,128]{2,1,0:T(8,128)(2,1)} %bitcast.4, bf16[128,128]{1,0:T(8,128)(2,1)} %long_ref.1, bf16[16,128]{1,0:T(8,128)(2,1)} %bitcast.8, bf16[256,2048]{1,0:T(8,128)(2,1)} %cot_ref.1), custom_call_target="tpu_custom_call" | custom-call | flops 6442450944 | bytes 8388608 | tf_op jit(solution)/shard_map/pallas_call | solution.py:433
  48.4 7.8 %shard_map.93 = (bf16[256,2048]{1,0:T(8,128)(2,1)}, bf16[3,256,2048]{2,1,0:T(8,128)(2,1)}, f32[128,128]{1,0:T(8,128)}, f32[16,128]{1,0:T(8,128)}, f32[3,7,128]{2,1,0:T(8,128)}) custom-call(bf16[16,256,128]{2,1,0:T(8,128)(2,1)} %get-tuple-element.13.gated_in, bf16[16,3,272,128]{3,2,1,0:T(8,128)(2,1)} %get-tuple-element.14.gm, ...), custom_call_target="tpu_custom_call" | custom-call | tf_op jit(solution)/shard_map/pallas_call | solution.py:476

commit v4 on v3

--- a/solution.py
+++ b/solution.py
@@ -27,8 +27,11 @@
         lax.broadcasted_iota(jnp.int32, (groups, LANES), 0)
         == lax.broadcasted_iota(jnp.int32, (groups, LANES), 1) // 16 + tile * 8
     ).astype(F32).astype(BF16)
-    for i in range(3):
-        out[i, :7] = jnp.dot(taps_ref[i], member, preferred_element_type=F32)
+    found = [jnp.dot(taps_ref[i], member, preferred_element_type=F32) for i in range(3)]
+    if out is not None:
+        for i in range(3):
+            out[i, :7] = found[i]
+    return found
 
 
 def circulant(row, shift):
@@ -301,10 +304,6 @@
                     (grad_inner * product).reshape(LANES // 8, 8, LANES), axis=0
                 )
 
-        @pl.when(has_prev)
-        def _():
-            gm_copy(t).start()
-
         red_in[t] = jnp.concatenate(folds, axis=0)
         red_in[tiles + t // 8, pl.ds(lax.rem(t, 8), 1)] = jnp.sum(skip, axis=0, keepdims=True)
         sums = []
@@ -321,9 +320,15 @@
             lax.broadcasted_iota(jnp.int32, (LANES, LANES), 0) // 16 + t * 8
             == lax.broadcasted_iota(jnp.int32, (LANES, LANES), 1)
         ).astype(F32)
-        return short_acc + jnp.dot(
+        short_acc = short_acc + jnp.dot(
             jnp.concatenate(sums, axis=0), member, precision=EXACT, preferred_element_type=F32
         )
+
+        @pl.when(has_prev)
+        def _():
+            gm_copy(t).start()
+
+        return short_acc
 
     skip_units = (tiles + 7) // 8
     red_in[tiles:] = jnp.zeros((units - tiles, 8, LANES), F32)
@@ -387,7 +392,6 @@
     skip_ref,
     short_ref,
     gmf,
-    taps,
 ):
     groups = long_ref.shape[0]
     tiles = groups // 8
@@ -402,7 +406,7 @@
 
     for u in range(step_tiles):
         cols = pl.ds(u * LANES, LANES)
-        tile_taps(taps_ref, pl.program_id(0) * step_tiles + u, taps)
+        taps = tile_taps(taps_ref, pl.program_id(0) * step_tiles + u, None)
         gated_ref[:, cols] = gated_in[u]
         for i in range(3):
             gmf[i] = gm[u, i].astype(F32)
@@ -410,7 +414,7 @@
             for i in range(3):
                 total = jnp.zeros((CHUNK, LANES), F32)
                 for j in range(7):
-                    total = total + taps[i, pl.ds(j, 1)] * gmf[
+                    total = total + taps[i][j : j + 1] * gmf[
                         i, pl.ds(start + j, CHUNK)
                     ]
                 fgrad_ref[i, pl.ds(start, CHUNK), cols] = total.astype(BF16)
@@ -498,7 +502,6 @@
         ),
         scratch_shapes=[
             pltpu.VMEM((3, rows + EDGE, LANES), F32),
-            pltpu.VMEM((3, 8, LANES), F32),
         ],
         compiler_params=pltpu.CompilerParams(vmem_limit_bytes=60 * 1024 * 1024),
     )(gated, grad_mixed, red, taps)

time: 56.4 us -> 52.1 us (0.924)
  Pallas kernels: 55.6 us -> 51.2 us
    pallas_call x1, Pallas kernels: 47.7 us -> 44.4 us  [body(): pl.pallas_call(functools.partial(kernel, n, tiles, rows, reduce_here), ou...]
    pallas_call x1, Pallas kernels: 7.83 us -> 6.8 us  [body(): pl.pallas_call(functools.partial(finish, step_tiles, rows, group_scale, t...]
where the time goes in v4:
time: 52.1 us; the launch traced here: 51.9 us
  Pallas kernels  51.2 us (98%)
  between operations  0.64 us (1%)
    pallas_call x1, Pallas kernels, body(): pl.pallas_call(functools.partial(kernel, n, tiles, rows, reduce_here), ou...  44.4 us
    pallas_call x1, Pallas kernels, body(): pl.pallas_call(functools.partial(finish, step_tiles, rows, group_scale, t...  6.8 us

profile of v4, /device:TPU:0, one launch (start us, length us, event | category | flops | bytes accessed | tf_op | source)
XLA Modules:
  0.0 51.9 jit_solution(14328308406588348494)
XLA Ops:
  0.6 44.4 %shard_map.92 = (bf16[16,256,128]{2,1,0:T(8,128)(2,1)}, bf16[16,3,272,128]{3,2,1,0:T(8,128)(2,1)}, f32[24,8,128]{2,1,0:T(8,128)}) custom-call(bf16[3,256,2048]{2,1,0:T(8,128)(2,1)} %feat_ref.1, bf16[3,7,128]{2,1,0:T(8,128)(2,1)} %bitcast.4, bf16[128,128]{1,0:T(8,128)(2,1)} %long_ref.1, bf16[16,128]{1,0:T(8,128)(2,1)} %bitcast.8, bf16[256,2048]{1,0:T(8,128)(2,1)} %cot_ref.1), custom_call_target="tpu_custom_call" | custom-call | flops 6442450944 | bytes 8388608 | tf_op jit(solution)/shard_map/pallas_call | solution.py:437
  45.1 6.8 %shard_map.93 = (bf16[256,2048]{1,0:T(8,128)(2,1)}, bf16[3,256,2048]{2,1,0:T(8,128)(2,1)}, f32[128,128]{1,0:T(8,128)}, f32[16,128]{1,0:T(8,128)}, f32[3,7,128]{2,1,0:T(8,128)}) custom-call(bf16[16,256,128]{2,1,0:T(8,128)(2,1)} %get-tuple-element.13.gated_in, bf16[16,3,272,128]{3,2,1,0:T(8,128)(2,1)} %get-tuple-element.14.gm, ...), custom_call_target="tpu_custom_call" | custom-call | tf_op jit(solution)/shard_map/pallas_call | solution.py:480
